TPU v7x, 32 devices: a whole 2x2x4 slice. The times are simulated.
32 devices in a mesh: grp: 2 (over y), col: 4 (over x, core), row: 4 (over z).
Axes of the slice: x: 2, y: 2, z: 4, core: 2. Of those that a mesh axis runs over, the one named last changes fastest.
Arguments:
- tokens: bfloat16 [1024, 7168], P(('grp', 'col'), 'row'), parts along dimension 0, may hold values from -6 to 6
- expert_ids: int32 [1024, 8], P(('grp', 'col')), parts along dimension 0, may hold values from 0 to 15, all different within a row; in each aligned block of 128 rows (0 to 127, 128 to 255, ...) at most 80 rows name the same one
- weight_index: int32 [1024, 8], P(('grp', 'col')), parts along dimension 0, may hold values from 0 to 63
- combine_table: float32 [64], replicated, may hold values from 0.1 to 1
- gate_weight: bfloat16 [16, 7168, 2048], P('col', None, 'row'), may hold values from -0.0625 to 0.0625
- up_weight: bfloat16 [16, 7168, 2048], P('col', None, 'row'), may hold values from -0.0625 to 0.0625
- down_weight: bfloat16 [16, 2048, 7168], P('col', None, 'row'), may hold values from -0.125 to 0.125
Outputs:
- layer_output: bfloat16 [1024, 7168], P(('grp', 'col'), 'row'), parts along dimension 0
There are 2 independent parts, one for each index of `grp`. A program takes and returns all parts, laid end to end along the dimension named above; an argument that names none is the same for every part. Nothing has to cross between parts.
Inputs may be any that keep to these rules, and one draw needn't show every extreme that they name: `expert_ids`: each row names 8 different experts, and every expert is named somewhere. Within the 128 rows of one index of col (aligned blocks), no expert is named by more than 80 rows.
All inputs are finite; a program needn't handle non-finite values.
Results may differ from a plain program's by a relative error of at most 0.0057.
Values may be sent and summed in bfloat16 or wider, within the bound.
A program may use at most 192 MiB of HBM per device.

v0:
```python
import jax
import jax.numpy as jnp
from jax import lax
from jax.sharding import PartitionSpec as P

CAP = 80


route_scale = 2.827


def slot_table(picked_ids, experts, capacity):
    count, picks = picked_ids.shape
    flat_ids = picked_ids.reshape(-1)
    one_hot = (flat_ids[:, None] == jnp.arange(experts, dtype=jnp.int32)[None, :]).astype(jnp.int32)
    ranking = jnp.sum((jnp.cumsum(one_hot, axis=0) - 1) * one_hot, axis=1)
    placing = flat_ids * capacity + ranking
    entries = jnp.arange(count * picks, dtype=jnp.int32) // picks
    holder = jnp.full((experts * capacity,), -1, jnp.int32).at[placing].set(entries)
    return (holder, placing)


def combine_weights(weight_index, combine_table):
    table_size = combine_table.shape[0]
    match = weight_index[..., None] == jnp.arange(table_size, dtype=jnp.int32)
    table_values = jnp.sum(jnp.where(match, combine_table, jnp.float32(0.0)), axis=-1)
    return route_scale * table_values / jnp.sum(table_values, axis=-1, keepdims=True)


def select_rows(source, holder, col_count, local_experts):
    is_valid = holder >= 0
    picked = jnp.take(source, jnp.maximum(holder, 0), axis=0)
    picked = jnp.where(is_valid[:, None], picked, jnp.zeros((), source.dtype))
    return picked.reshape(col_count, local_experts, CAP, source.shape[1])


def shards(tokens, expert_ids, weight_index, combine_table, gate_weight, up_weight, down_weight):
    col_count = lax.axis_size("col")
    local_experts = gate_weight.shape[0]
    experts = local_experts * col_count
    holder, placing = slot_table(expert_ids, experts, CAP)
    full_tokens = lax.all_gather(tokens, "row", axis=1, tiled=True)
    outgoing = select_rows(full_tokens, holder, col_count, local_experts)
    arrived = lax.all_to_all(outgoing, "col", split_axis=0, concat_axis=0, tiled=True)
    gate_part = jnp.einsum(
        "secw,ewf->secf", arrived, gate_weight, preferred_element_type=jnp.float32
    )
    up_part = jnp.einsum("secw,ewf->secf", arrived, up_weight, preferred_element_type=jnp.float32)
    hidden = (jax.nn.silu(gate_part) * up_part).astype(jnp.bfloat16)
    expert_out = jnp.einsum(
        "secf,efd->secd",
        lax.all_gather(hidden, "row", axis=3, tiled=True),
        down_weight,
        preferred_element_type=jnp.float32,
    ).astype(jnp.bfloat16)
    returned = lax.all_to_all(expert_out, "col", split_axis=0, concat_axis=0, tiled=True)
    features = returned.shape[3]
    gathered = jnp.take(returned.reshape(experts * CAP, features), placing, axis=0)
    gathered = gathered.reshape(expert_ids.shape + (features,)).astype(jnp.float32)
    weights = combine_weights(weight_index, combine_table)
    return jnp.sum(weights[..., None] * gathered, axis=1).astype(jnp.bfloat16)


def solution(mesh):
    in_specs = (
        P(("grp", "col"), "row"),
        P(("grp", "col"), None),
        P(("grp", "col"), None),
        P(),
        P("col", None, "row"),
        P("col", None, "row"),
        P("col", None, "row"),
    )
    out_specs = P(("grp", "col"), "row")
    return jax.shard_map(shards, mesh=mesh, in_specs=in_specs, out_specs=out_specs, check_vma=False)
```

profile of v0, /device:TPU:0, one launch (start us, length us, event | category | flops | bytes accessed | tf_op | source)
XLA Modules:
  0.0 540.2 jit_solution(3506763081963057486)
XLA Ops:
  6.5 0.0 all-gather.3.cloned.1.call-start
  6.5 0.7 all-gather.3.cloned.1.call-update
  7.3 0.0 all-gather.5.cloned.1.call-start
  7.3 0.8 copy.41
  8.1 0.1 eq.42
  8.2 0.1 reshape.105
  8.3 4.5 reduce-window.6
  12.8 0.1 slice.12
  12.9 0.1 copy.43
  13.1 0.1 copy.44
  13.1 0.7 broadcast_multiply_fusion
  13.8 0.1 copy.47
  13.9 0.1 mul.53
  14.0 0.1 add_add_fusion
  14.2 0.0 copy-start
  14.2 0.6 copy-done
  14.7 4.3 scatter_custom_fusion
  19.1 0.1 broadcast_in_dim.60
  19.2 0.1 broadcast_in_dim.62
  19.3 33.8 %all-gather.3.cloned.1.call-done = bf16[128,7168]{1,0:T(8,128)(2,1)} async-done(((bf16[128,1792]{1,0:T(8,128)(2,1)}), bf16[128,7168]{1,0:T(8,128)(2,1)}) %all-gather.3.cloned.1.call-update) | async-done | bytes 1835024 | tf_op jit(solution)/shard_map/all_gather | solution.py:42
  53.1 32.6 %gather_fusion = bf16[1280,7168]{1,0:T(8,128)(2,1)} fusion(bf16[128,7168]{1,0:T(8,128)(2,1)} %all-gather.3.cloned.1.call-done, s32[2048]{0:T(1024)S(1)} %pad_clamp_fusion), kind=kCustom, calls=%fused_computation | custom fusion | bytes 36705280 | tf_op jit(solution)/shard_map/jit(_take)/gather | solution.py:32
  85.7 0.0 copy-done.3
  85.7 9.1 %select_select_fusion = bf16[4,4,80,7168]{3,2,1,0:T(8,128)(2,1)S(1)} fusion(bf16[4,4,80,7168]{3,2,1,0:T(8,128)(2,1)} %bitcast.61, pred[4,4,80]{2,1,0:T(4,128)(4,1)S(1)} %broadcast_in_dim.62, pred[4,4,80]{2,1,0:T(4,128)(4,1)S(1)} %broadcast_in_dim.60), kind=kLoop, calls=%fused_computation.9 | loop fusion | flops 18350080 | bytes 36702720 | tf_op jit(solution)/shard_map/jit(_where)/select_n | solution.py:33
  94.8 204.3 %all_to_all.10 = bf16[4,4,80,7168]{3,2,1,0:T(8,128)(2,1)} all-to-all(bf16[4,4,80,7168]{3,2,1,0:T(8,128)(2,1)S(1)} %select_select_fusion), channel_id=1, replica_groups=mesh['grp'=2,'col'=4,'row'=4] {'col'}, dimensions={0} | all-to-all | bytes 36700160 | tf_op jit(solution)/shard_map/all_to_all | solution.py:44
  299.2 19.0 %fusion.2 = f32[4,4,80,512]{3,2,1,0:T(8,128)S(1)} fusion(bf16[4,7168,512]{2,1,0:T(8,128)(2,1)} %param.12, bf16[4,4,80,7168]{3,2,1,0:T(8,128)(2,1)} %all_to_all.10), kind=kOutput, calls=%fused_computation.5 | convolution fusion | flops 9395240960 | bytes 50331648 | tf_op jit(solution)/shard_map/secw,ewf->secf/dot_general | solution.py:48
  318.2 24.7 %fusion.10 = bf16[4,4,80,512]{3,2,0,1:T(8,128)(2,1)} fusion(f32[4,4,80,512]{3,2,1,0:T(8,128)S(1)} %fusion.2, bf16[4,7168,512]{2,1,0:T(8,128)(2,1)} %param.11, bf16[4,4,80,7168]{3,2,1,0:T(8,128)(2,1)} %all_to_all.10), kind=kOutput, calls=%fused_computation.16 | convolution fusion | flops 9399173120 | bytes 51642368 | tf_op jit(solution)/shard_map/secw,ewf->secf/dot_general | solution.py:45
  342.9 0.0 all-gather.5.cloned.1.call-update
  343.0 96.2 %all-gather.5.cloned.1.call-done = bf16[4,4,80,2048]{3,2,0,1:T(8,128)(2,1)} async-done(((bf16[4,4,80,512]{3,2,0,1:T(8,128)(2,1)}), bf16[4,4,80,2048]{3,2,0,1:T(8,128)(2,1)}) %all-gather.5.cloned.1.call-update) | async-done | bytes 5242896 | tf_op jit(solution)/shard_map/all_gather | solution.py:52
  439.1 18.0 %convert_bitcast_fusion = bf16[4,4,80,1792]{3,2,0,1:T(8,128)(2,1)S(1)} fusion(bf16[4,4,80,2048]{3,2,0,1:T(8,128)(2,1)} %all-gather.5.cloned.1.call-done, bf16[4,2048,1792]{2,1,0:T(8,128)(2,1)} %param.13), kind=kOutput, calls=%fused_computation.13 | convolution fusion | flops 9397534720 | bytes 39190528 | tf_op jit(solution)/shard_map/secf,efd->secd/dot_general | solution.py:50
  457.1 0.0 copy-start.1
  457.2 0.0 copy-start.2
  457.2 0.0 copy-start.5
  457.2 0.0 copy-start.6
  457.2 0.0 copy-start.4
  457.2 2.5 copy.50
  459.7 5.1 all-to-all-start.1
  464.8 0.0 copy-done.1
  464.8 0.1 reduce_sum.43
  464.9 0.0 copy-done.2
  465.0 0.1 copy.46
  465.1 0.0 copy-done.5
  465.1 0.0 copy-done.6
  465.1 0.2 select_reduce_fusion
  465.3 0.1 copy.40
  465.4 0.0 copy-done.4
  465.4 51.6 %all-to-all-done.1 = bf16[4,4,80,1792]{3,2,1,0:T(8,128)(2,1)} async-done(((bf16[4,4,80,1792]{3,2,1,0:T(8,128)(2,1)}), bf16[4,4,80,1792]{3,2,1,0:T(8,128)(2,1)}, u32[]{:S(2)}, u32[]{:S(2)}) %all-to-all-start.1) | async-done | bytes 4587552 | tf_op jit(solution)/shard_map/all_to_all | solution.py:56
  517.0 10.8 %gather_fusion.1 = bf16[1024,1792]{1,0:T(8,128)(2,1)} fusion(bf16[1280,1792]{1,0:T(8,128)(2,1)} %bitcast.14, s32[1024]{0:T(1024)S(1)} %broadcast_clamp_fusion), kind=kCustom, calls=%fused_computation.1 | custom fusion | bytes 7344128 | tf_op jit(solution)/shard_map/jit(_take)/gather | solution.py:58
  527.8 5.6 %multiply_reduce_fusion = bf16[128,1792]{1,0:T(8,128)(2,1)} fusion(bf16[1024,1792]{1,0:T(8,128)(2,1)} %gather_fusion.1, f32[128,8]{1,0:T(8,128)S(1)} %copy.40, pred[128,8]{1,0:T(8,128)(4,1)S(1)} %copy.46), kind=kLoop, calls=%fused_computation.12 | loop fusion | flops 7110656 | bytes 4133888 | tf_op jit(solution)/shard_map/reduce_sum | solution.py:61
  (14 shorter events, 0.2 us)
Async XLA Ops:
  6.5 46.5 %all-gather.3.cloned.1.call-start = ((), (), s32[]{:S(2)}) async-start(), calls=%async_computation.2 | async-start | bytes 2293760 | tf_op jit(solution)/shard_map/all_gather | solution.py:42
  7.3 431.9 %all-gather.5.cloned.1.call-start = ((), (), s32[]{:S(2)}) async-start(), calls=%async_computation.3 | async-start | bytes 6553600 | tf_op jit(solution)/shard_map/all_gather | solution.py:52
  14.2 0.6 copy-start
  14.7 71.0 %copy-start.3 = (s32[1024,1]{0,1:T(1,128)}, s32[1024,1]{0,1:T(1,128)S(1)}, u32[]{:S(2)}) copy-start(s32[1024,1]{0,1:T(1,128)S(1)} %compare_select_fusion) | copy-start | bytes 12292
  457.1 7.7 %copy-start.1 = (s32[1024]{0:T(1024)S(1)}, s32[1024]{0:T(1024)}, u32[]{:S(2)}) copy-start(s32[1024]{0:T(1024)} %copy-done) | copy-start | bytes 12292
  457.2 7.8 %copy-start.2 = (s32[128,8]{0,1:T(8,128)S(1)}, s32[128,8]{0,1:T(8,128)}, u32[]{:S(2)}) copy-start(s32[128,8]{0,1:T(8,128)} %param.8) | copy-start | bytes 12292
  457.2 7.9 %copy-start.5 = (s32[128,8]{0,1:T(8,128)S(1)}, s32[128,8]{0,1:T(8,128)}, u32[]{:S(2)}) copy-start(s32[128,8]{0,1:T(8,128)} %param.9) | copy-start | bytes 12292
  457.2 7.9 %copy-start.6 = (f32[64]{0:T(128)S(1)}, f32[64]{0:T(128)}, u32[]{:S(2)}) copy-start(f32[64]{0:T(128)} %param.10) | copy-start | bytes 772
  457.2 8.2 %copy-start.4 = (s32[1024,1]{0,1:T(1,128)S(1)}, s32[1024,1]{0,1:T(1,128)}, u32[]{:S(2)}) copy-start(s32[1024,1]{0,1:T(1,128)} %copy-done.3) | copy-start | bytes 12292
  459.7 57.4 %all-to-all-start.1 = ((bf16[4,4,80,1792]{3,2,1,0:T(8,128)(2,1)}), bf16[4,4,80,1792]{3,2,1,0:T(8,128)(2,1)}, u32[]{:S(2)}, u32[]{:S(2)}) async-start(bf16[4,4,80,1792]{3,2,1,0:T(8,128)(2,1)} %copy.50), calls=%async_computation.1 | async-start | bytes 9175040 | tf_op jit(solution)/shard_map/all_to_all | solution.py:56
Sparse Core Ops, SparseCore 0:
  8.9 44.0 all-gather.2
  343.1 96.0 all-gather.4
where the time goes:
time: 541 us; the launch traced here: 540 us
  blocking collectives  204 us (38%)
  waiting for transfers between devices  182 us (34%)
  matrix products  61.8 us (11%)
  local copies, waits for them, and re-layouts  52.8 us (10%)
  other arithmetic  20.2 us (4%)
  between operations  13.6 us (3%)
    all_to_all x1, blocking collectives, shards(): lax.all_to_all(outgoing, 'col', split_axis=0, concat_axis=0, tiled=True)  204 us
    all_gather x1, waiting for transfers between devices, shards(): lax.all_gather(hidden, 'row', axis=3, tiled=True)  96.2 us
    all_to_all x1, waiting for transfers between devices, shards(): lax.all_to_all(expert_out, 'col', split_axis=0, concat_axis=0, tiled=True)  51.6 us
    all_gather x1, waiting for transfers between devices, shards(): full_tokens = lax.all_gather(tokens, 'row', axis=1, tiled=True)  33.8 us
    gather x1, local copies, waits for them, and re-layouts, select_rows(): picked = jnp.take(source, jnp.maximum(holder, 0), axis=0)  32.6 us
    dot_general x1, matrix products, shards(): jnp.einsum('secw,ewf->secf', arrived, gate_weight, preferred_element_type...  24.7 us
    dot_general x1, matrix products, shards(): jnp.einsum('secw,ewf->secf', arrived, up_weight, preferred_element_type=j...  19 us
    dot_general x1, matrix products, shards(): jnp.einsum('secf,efd->secd', lax.all_gather(hidden, 'row', axis=3, tiled=...  18 us
  transfers between devices with their start and end apart: 3, of which 3 were waited for; matrix products, arithmetic and copies ran while one was open for 2% of the time, Pallas kernels for 0%

commit v1 on v0

--- a/solution.py
+++ b/solution.py
@@ -1,6 +1,10 @@
+import functools
+
 import jax
 import jax.numpy as jnp
 from jax import lax
+from jax.experimental import pallas as pl
+from jax.experimental.pallas import tpu as pltpu
 from jax.sharding import PartitionSpec as P
 
 CAP = 80
@@ -34,7 +38,7 @@
     return picked.reshape(col_count, local_experts, CAP, source.shape[1])
 
 
-def shards(tokens, expert_ids, weight_index, combine_table, gate_weight, up_weight, down_weight):
+def plain_shards(tokens, expert_ids, weight_index, combine_table, gate_weight, up_weight, down_weight):
     col_count = lax.axis_size("col")
     local_experts = gate_weight.shape[0]
     experts = local_experts * col_count
@@ -61,6 +65,353 @@
     return jnp.sum(weights[..., None] * gathered, axis=1).astype(jnp.bfloat16)
 
 
+TILE = 256
+VMEM_BYTES = 60 * 1024 * 1024
+MESH = pl.DeviceIdType.MESH
+
+
+def expert_kernel(
+    geometry, tok_hbm, meta_ref, table_ref, gate_hbm, up_hbm, down_hbm, out_ref,
+    tok_all, meta_all, gate_buf, up_buf, down_buf, acc_gate, acc_up, place, spread, slot_weight,
+    hid, acc, part, sib_in, x_out, x_in,
+    local_sem, gate_sem, up_sem, down_sem, meta_send, meta_recv, tok_send, tok_recv,
+    hid_send, hid_recv, part_send, part_recv,
+):
+    cols, rows, count, picks, local, width, hidden, table = geometry
+    slots = cols * CAP
+    chunks = hidden // TILE
+    g = lax.axis_index("grp")
+    c = lax.axis_index("col")
+    r = lax.axis_index("row")
+    core, chip = c % 2, c // 2
+    col_of = [c, 2 * chip + 1 - core, 2 * (1 - chip) + core, 2 * (1 - chip) + 1 - core]
+    has_up, has_down = r < rows - 1, r > 0
+
+    def remote(src, dst, send, recv, col, row):
+        return pltpu.make_async_remote_copy(
+            src_ref=src, dst_ref=dst, send_sem=send, recv_sem=recv,
+            device_id=(g, col, row), device_id_type=MESH,
+        )
+
+    def block(q, s):
+        return tok_all.at[q, pl.ds(pl.multiple_of(s * count, count), count), :]
+
+    def tok_copy(kind, q):
+        s = col_of[2] if kind == 4 else c
+        col = (c, c, col_of[1], col_of[2], col_of[1])[kind]
+        row = (r + 1, r - 1, r, r, r)[kind]
+        relation = (0, 0, 1, 2, 3)[kind]
+        return remote(block(q, s), block(q, s), tok_send.at[kind, q], tok_recv.at[relation, q], col, row)
+
+    def tok_wait(relation, q):
+        view = block(q, col_of[relation])
+        remote(view, view, tok_send.at[0, q], tok_recv.at[relation, q], c, r).wait_recv()
+
+    def hid_copy(direction, e, q):
+        view = hid.at[e, q]
+        return remote(
+            view, view, hid_send.at[direction, e, q], hid_recv.at[e, q], c, (r + 1, r - 1)[direction]
+        )
+
+    def weight_copies(e, n):
+        cut = pl.ds(pl.multiple_of(n * TILE, TILE), TILE)
+        return (
+            pltpu.make_async_copy(gate_hbm.at[e, :, cut], gate_buf.at[n], gate_sem.at[n]),
+            pltpu.make_async_copy(up_hbm.at[e, :, cut], up_buf.at[n], up_sem.at[n]),
+        )
+
+    def down_copy(e, slot):
+        return pltpu.make_async_copy(down_hbm.at[e], down_buf.at[slot], down_sem.at[slot])
+
+    local_copy = pltpu.make_async_copy(tok_hbm, block(r, c), local_sem)
+    local_copy.start()
+    for n in range(chunks):
+        for copy in weight_copies(0, n):
+            copy.start()
+    for e in range(min(2, local)):
+        down_copy(e, e).start()
+
+    barrier = pltpu.get_barrier_semaphore()
+    for k in (1, 2, 3):
+        pl.semaphore_signal(barrier, inc=1, device_id=(g, col_of[k], r), device_id_type=MESH)
+
+    @pl.when(has_up)
+    def _():
+        pl.semaphore_signal(barrier, inc=1, device_id=(g, c, r + 1), device_id_type=MESH)
+
+    @pl.when(has_down)
+    def _():
+        pl.semaphore_signal(barrier, inc=1, device_id=(g, c, r - 1), device_id_type=MESH)
+
+    pl.semaphore_wait(barrier, 3 + jnp.where(has_up, 1, 0) + jnp.where(has_down, 1, 0))
+
+    def meta_copy(k):
+        return remote(meta_ref, meta_all.at[c], meta_send.at[k - 1], meta_recv.at[k - 1], col_of[k], r)
+
+    for k in (1, 2, 3):
+        meta_copy(k).start()
+    local_copy.wait()
+
+    def spread_tokens(q, upward, downward):
+        @pl.when(upward)
+        def _():
+            tok_copy(0, q).start()
+
+        @pl.when(downward)
+        def _():
+            tok_copy(1, q).start()
+
+        tok_copy(3, q).start()
+        tok_copy(2, q).start()
+
+    spread_tokens(r, has_up, has_down)
+
+    meta_all[c] = meta_ref[...]
+    acc[...] = jnp.zeros_like(acc)
+    for k in (1, 2, 3):
+        view = meta_all.at[col_of[k]]
+        remote(meta_ref, view, meta_send.at[k - 1], meta_recv.at[k - 1], c, r).wait_recv()
+    before = (
+        lax.broadcasted_iota(jnp.int32, (count, count), 0)
+        < lax.broadcasted_iota(jnp.int32, (count, count), 1)
+    ).astype(jnp.float32).astype(jnp.bfloat16)
+    line = lax.broadcasted_iota(jnp.int32, (count, count), 0).astype(jnp.float32)
+
+    @pl.loop(0, cols)
+    def _(s):
+        ids = meta_all[s, 0:picks, :]
+        index = meta_all[s, picks:2 * picks, :]
+        values = lax.fori_loop(
+            0, table, lambda j, v: jnp.where(index == j, table_ref[j], v),
+            jnp.zeros((picks, count), jnp.float32),
+        )
+        weights = route_scale * values / jnp.sum(values, axis=0, keepdims=True)
+        for e in range(local):
+            match = ids == c * local + e
+            named = jnp.sum(jnp.where(match, 1.0, 0.0), axis=0, keepdims=True)
+            weight = jnp.sum(jnp.where(match, weights, 0.0), axis=0, keepdims=True)
+            wide = jnp.broadcast_to(named, (16, count)).astype(jnp.bfloat16)
+            rank = jnp.dot(wide, before, preferred_element_type=jnp.float32)[0:1, :]
+            rank = jnp.where(named > 0.5, rank, -1.0)
+            chosen = jnp.where(line == rank, 1.0, 0.0)
+            place[e, s] = chosen[:CAP].astype(jnp.bfloat16)
+            spread[e, s] = chosen.T.astype(jnp.bfloat16)
+            scale = jnp.sum(chosen[:CAP] * weight, axis=1, keepdims=True)
+            slot_weight[e, s] = jnp.broadcast_to(scale, (CAP, 128))
+
+    for d in range(1, rows + 1):
+        for sign in (-1, 1):
+            q = r + sign * d
+            if d < rows:
+                @pl.when((q >= 0) & (q < rows))
+                def _():
+                    tok_wait(0, q)
+                    spread_tokens(q, has_up & (q < r), has_down & (q > r))
+
+            p = r + sign * (d - 1)
+            if d > 1 or sign < 0:
+                @pl.when((p >= 0) & (p < rows))
+                def _():
+                    tok_wait(2, p)
+                    tok_copy(4, p).start()
+    for q in range(rows):
+        tok_wait(1, q)
+        tok_wait(3, q)
+
+    def project(e):
+        @pl.loop(0, chunks)
+        def _(n):
+            for copy in weight_copies(e, n):
+                copy.wait()
+            acc_gate[...] = jnp.zeros_like(acc_gate)
+            acc_up[...] = jnp.zeros_like(acc_up)
+
+            @pl.loop(0, rows)
+            def _(j):
+                depth = pl.ds(pl.multiple_of(j * width, width), width)
+                x = tok_all[j]
+                acc_gate[...] += jnp.dot(x, gate_buf[n, depth, :], preferred_element_type=jnp.float32)
+                acc_up[...] += jnp.dot(x, up_buf[n, depth, :], preferred_element_type=jnp.float32)
+
+            @pl.when(e + 1 < local)
+            def _():
+                for copy in weight_copies(e + 1, n):
+                    copy.start()
+
+            cut = pl.ds(pl.multiple_of(n * TILE, TILE), TILE)
+            for s in range(cols):
+                span = pl.ds(s * count, count)
+                v = acc_gate[span, :]
+                h = (v / (1.0 + jnp.exp(-v)) * acc_up[span, :]).astype(jnp.bfloat16)
+                picked = jnp.dot(place[e, s], h, preferred_element_type=jnp.float32)
+                hid[e, r, pl.ds(s * CAP, CAP), cut] = picked.astype(jnp.bfloat16)
+
+        @pl.when(has_up)
+        def _():
+            hid_copy(0, e, r).start()
+
+        @pl.when(has_down)
+        def _():
+            hid_copy(1, e, r).start()
+
+    def forward(e, d):
+        for sign in (-1, 1):
+            q = r + sign * d
+
+            @pl.when((q >= 0) & (q < rows))
+            def _():
+                view = hid.at[e, q]
+                remote(view, view, hid_send.at[0, e, q], hid_recv.at[e, q], c, r).wait_recv()
+
+                @pl.when(has_up if sign < 0 else has_down)
+                def _():
+                    hid_copy(0 if sign < 0 else 1, e, q).start()
+
+    def finish(e):
+        slot = e % 2
+        down_copy(e, slot).wait()
+
+        @pl.loop(0, width // TILE)
+        def _(n):
+            cut = pl.ds(pl.multiple_of(n * TILE, TILE), TILE)
+            full = sum(
+                jnp.dot(
+                    hid[e, q], down_buf[slot, pl.ds(q * hidden, hidden), cut],
+                    preferred_element_type=jnp.float32,
+                )
+                for q in range(rows)
+            )
+            for s in range(cols):
+                scaled = full[s * CAP:(s + 1) * CAP] * slot_weight[e, s][:, 0:1]
+                back = jnp.dot(
+                    spread[e, s][:, :CAP], scaled.astype(jnp.bfloat16), preferred_element_type=jnp.float32
+                )
+                acc[pl.ds(s * count, count), cut] += back
+
+        @pl.when(e + 2 < local)
+        def _():
+            down_copy(e + 2, slot).start()
+
+    @pl.loop(0, local + rows - 1)
+    def _(k):
+        @pl.when(k < local)
+        def _():
+            project(k)
+
+        for d in range(1, rows):
+            @pl.when((k >= d) & (k - d < local))
+            def _():
+                forward(k - d, d)
+
+        @pl.when(k >= rows - 1)
+        def _():
+            finish(k - (rows - 1))
+
+    def mine(k):
+        return acc[pl.ds(pl.multiple_of(col_of[k] * count, count), count), :]
+
+    def part_copy(i):
+        src = (part.at[0], part.at[1], x_out)[i]
+        dst = (sib_in.at[0], sib_in.at[1], x_in)[i]
+        return remote(src, dst, part_send.at[i], part_recv.at[i], col_of[2 if i == 2 else 1], r)
+
+    part[0] = mine(3).astype(jnp.bfloat16)
+    part_copy(0).start()
+    part[1] = mine(1).astype(jnp.bfloat16)
+    part_copy(1).start()
+    part_copy(0).wait_recv()
+    x_out[...] = (mine(2) + sib_in[0].astype(jnp.float32)).astype(jnp.bfloat16)
+    part_copy(2).start()
+    part_copy(1).wait_recv()
+    part_copy(2).wait_recv()
+    total = mine(0) + sib_in[1].astype(jnp.float32) + x_in[...].astype(jnp.float32)
+    out_ref[...] = total.astype(out_ref.dtype)
+
+    for i in range(3):
+        part_copy(i).wait_send()
+        meta_copy(i + 1).wait_send()
+    for q in range(rows):
+        for kind in range(5):
+            if kind >= 2:
+                tok_copy(kind, q).wait_send()
+            else:
+                @pl.when((has_up & (q <= r)) if kind == 0 else (has_down & (q >= r)))
+                def _():
+                    tok_copy(kind, q).wait_send()
+                    for e in range(local):
+                        hid_copy(kind, e, q).wait_send()
+
+
+def scratch(geometry):
+    cols, rows, count, picks, local, width, hidden, table = geometry
+    slots, chunks = cols * CAP, hidden // TILE
+    bf16, f32 = jnp.bfloat16, jnp.float32
+    return [
+        ((rows, cols * count, width), bf16),
+        ((cols, 2 * picks, count), jnp.int32),
+        ((chunks, rows * width, TILE), bf16),
+        ((chunks, rows * width, TILE), bf16),
+        ((2, rows * hidden, width), bf16),
+        ((cols * count, TILE), f32),
+        ((cols * count, TILE), f32),
+        ((local, cols, CAP, count), bf16),
+        ((local, cols, count, count), bf16),
+        ((local, cols, CAP, 128), f32),
+        ((local, rows, slots, hidden), bf16),
+        ((cols * count, width), f32),
+        ((2, count, width), bf16),
+        ((2, count, width), bf16),
+        ((count, width), bf16),
+        ((count, width), bf16),
+    ]
+
+
+def kernel_shards(tokens, expert_ids, weight_index, combine_table, gate_weight, up_weight, down_weight):
+    cols, rows = lax.axis_size("col"), lax.axis_size("row")
+    count, picks = expert_ids.shape
+    local, depth, hidden = gate_weight.shape
+    geometry = (cols, rows, count, picks, local, tokens.shape[1], hidden, combine_table.shape[0])
+    chunks = hidden // TILE
+    meta = jnp.concatenate([expert_ids.T, weight_index.T], axis=0)
+    dma = pltpu.SemaphoreType.DMA
+    anywhere = pl.BlockSpec(memory_space=pl.ANY)
+    slots = cols * CAP
+    flops = 4 * cols * count * depth * hidden * local + 2 * slots * rows * hidden * tokens.shape[1] * local
+    moved = 2 * (gate_weight.size + up_weight.size + down_weight.size)
+    return pl.pallas_call(
+        functools.partial(expert_kernel, geometry),
+        out_shape=jax.ShapeDtypeStruct(tokens.shape, jnp.bfloat16),
+        in_specs=[
+            anywhere,
+            pl.BlockSpec(memory_space=pltpu.VMEM),
+            pl.BlockSpec(memory_space=pltpu.SMEM),
+            anywhere, anywhere, anywhere,
+        ],
+        out_specs=pl.BlockSpec(memory_space=pltpu.VMEM),
+        scratch_shapes=[pltpu.VMEM(shape, kind) for shape, kind in scratch(geometry)] + [
+            dma, dma((chunks,)), dma((chunks,)), dma((2,)),
+            dma((3,)), dma((3,)), dma((5, rows)), dma((4, rows)),
+            dma((2, local, rows)), dma((local, rows)), dma((3,)), dma((3,)),
+        ],
+        compiler_params=pltpu.CompilerParams(
+            collective_id=0, has_side_effects=True, vmem_limit_bytes=VMEM_BYTES
+        ),
+        cost_estimate=pl.CostEstimate(flops=flops, bytes_accessed=moved, transcendentals=0),
+    )(tokens, meta, combine_table, gate_weight, up_weight, down_weight)
+
+
+def shards(tokens, expert_ids, weight_index, combine_table, gate_weight, up_weight, down_weight):
+    cols, rows = lax.axis_size("col"), lax.axis_size("row")
+    count, picks = expert_ids.shape
+    local, depth, hidden = gate_weight.shape
+    width = tokens.shape[1]
+    geometry = (cols, rows, count, picks, local, width, hidden, combine_table.shape[0])
+    held = sum(jnp.dtype(kind).itemsize * functools.reduce(lambda a, b: a * b, shape) for shape, kind in scratch(geometry))
+    fits = cols == 4 and hidden % TILE == 0 and width % TILE == 0 and count % 128 == 0 and held < VMEM_BYTES * 9 // 10
+    form = kernel_shards if fits else plain_shards
+    return form(tokens, expert_ids, weight_index, combine_table, gate_weight, up_weight, down_weight)
+
+
 def solution(mesh):
     in_specs = (
         P(("grp", "col"), "row"),

time: 541 us -> 174 us (0.32)
  blocking collectives: 204 us -> 0 us
  waiting for transfers between devices: 182 us -> 0 us
  Pallas kernels: 0 us -> 171 us
  matrix products: 61.8 us -> 0 us
  local copies, waits for them, and re-layouts: 52.8 us -> 1.82 us
  other arithmetic: 20.2 us -> 1.32 us
  between operations: 13.6 us -> 0.01 us
    all_to_all x1 -> x0, blocking collectives: 204 us -> none  [shards(): lax.all_to_all(outgoing, 'col', split_axis=0, concat_axis=0, tiled=True)]
    pallas_call x0 -> x1, Pallas kernels: none -> 171 us  [kernel_shards(): pl.pallas_call(functools.partial(expert_kernel, geometry), out_shape=jax....]
    all_gather x2 -> x0, waiting for transfers between devices: 130 us -> none  [the longest x1 96.2 us: shards(): lax.all_gather(hidden, 'row', axis=3, tiled=True)]
    dot_general x3 -> x0, matrix products: 61.8 us -> none  [the longest x1 24.7 us: shards(): jnp.einsum('secw,ewf->secf', arrived, gate_weight, preferred_element_type...]
    all_to_all x1 -> x0, waiting for transfers between devices: 51.6 us -> none  [shards(): lax.all_to_all(expert_out, 'col', split_axis=0, concat_axis=0, tiled=True)]
    gather x2 -> x0, local copies, waits for them, and re-layouts: 43.5 us -> none  [the longest x1 32.6 us: select_rows(): picked = jnp.take(source, jnp.maximum(holder, 0), axis=0)]
    select_n x3 -> x0, other arithmetic: 9.11 us -> none  [the longest x1 9.1 us: select_rows(): picked = jnp.where(is_valid[:, None], picked, jnp.zeros((), source.dtype))]
    reduce_sum x3 -> x0, other arithmetic: 5.75 us -> none  [the longest x1 5.56 us: shards(): return jnp.sum(weights[..., None] * gathered, axis=1).astype(jnp.bfloat16)]
  transfers between devices with their start and end apart: 3 -> 0, of which waited for: 3 -> 0; matrix products, arithmetic and copies ran while one was open for 2% -> 0% of each run, Pallas kernels for 0% -> 0%
where the time goes in v1:
time: 174 us
  Pallas kernels  171 us (98%)
  local copies, waits for them, and re-layouts  1.82 us (1%)
    pallas_call x1, Pallas kernels, kernel_shards(): pl.pallas_call(functools.partial(expert_kernel, geometry), out_shape=jax....  171 us

profile of v1, /device:TPU:0, one launch (start us, length us, event | category | flops | bytes accessed | tf_op | source)
XLA Modules:
  0.0 174.2 jit_solution(13173001808291714153)
XLA Ops:
  0.0 1.3 pad_add_fusion.meta_ref
  1.3 171.0 %shard_map.73 = bf16[128,1792]{1,0:T(8,128)(2,1)} custom-call(bf16[128,1792]{1,0:T(8,128)(2,1)} %tok_hbm.1, s32[16,128]{1,0:T(8,128)} %pad_add_fusion.meta_ref, f32[64]{0:T(128)} %table_ref.1, bf16[4,7168,512]{2,1,0:T(8,128)(2,1)} %gate_hbm.1, bf16[4,7168,512]{2,1,0:T(8,128)(2,1)} %up_hbm.1, bf16[4,2048,1792]{2,1,0:T(8,128)(2,1)} %down_hbm.1), custom_call_target="tpu_custom_call" | custom-call | flops 39460012032 | bytes 88080384 | tf_op jit(solution)/shard_map/pallas_call | solution.py:381
  172.4 1.8 %copy.9 = bf16[128,1792]{1,0:T(8,128)(2,1)} copy(bf16[128,1792]{1,0:T(8,128)(2,1)} %shard_map.73) | data formatting | bytes 917504

commit v2 on v1

--- a/solution.py
+++ b/solution.py
@@ -78,8 +78,9 @@
     hid_send, hid_recv, part_send, part_recv,
 ):
     cols, rows, count, picks, local, width, hidden, table = geometry
-    slots = cols * CAP
+    slots = cols * CAP // 2
     chunks = hidden // TILE
+    units = 2 * local
     g = lax.axis_index("grp")
     c = lax.axis_index("col")
     r = lax.axis_index("row")
@@ -199,113 +200,118 @@
             scale = jnp.sum(chosen[:CAP] * weight, axis=1, keepdims=True)
             slot_weight[e, s] = jnp.broadcast_to(scale, (CAP, 128))
 
-    for d in range(1, rows + 1):
+    for d in range(1, rows):
         for sign in (-1, 1):
             q = r + sign * d
-            if d < rows:
-                @pl.when((q >= 0) & (q < rows))
-                def _():
-                    tok_wait(0, q)
-                    spread_tokens(q, has_up & (q < r), has_down & (q > r))
-
-            p = r + sign * (d - 1)
-            if d > 1 or sign < 0:
-                @pl.when((p >= 0) & (p < rows))
-                def _():
-                    tok_wait(2, p)
-                    tok_copy(4, p).start()
+
+            @pl.when((q >= 0) & (q < rows))
+            def _():
+                tok_wait(0, q)
+                spread_tokens(q, has_up & (q < r), has_down & (q > r))
     for q in range(rows):
         tok_wait(1, q)
-        tok_wait(3, q)
-
-    def project(e):
+
+    def pass_on(d):
+        for sign in (-1, 1) if d > 0 else (1,):
+            q = r + sign * d
+
+            @pl.when((q >= 0) & (q < rows))
+            def _():
+                tok_wait(2, q)
+                tok_copy(4, q).start()
+
+    def chip_of(u):
+        own = (u == 0) | ((u >= 2) & (u % 2 == 1))
+        return jnp.where(own, chip, 1 - chip)
+
+    def project(u):
+        e, h = u // 2, u % 2
+        first = 2 * chip_of(u)
+        span = pl.ds(pl.multiple_of(first * count, 2 * count), 2 * count)
+
         @pl.loop(0, chunks)
         def _(n):
-            for copy in weight_copies(e, n):
-                copy.wait()
+            @pl.when(h == 0)
+            def _():
+                for copy in weight_copies(e, n):
+                    copy.wait()
+
             acc_gate[...] = jnp.zeros_like(acc_gate)
             acc_up[...] = jnp.zeros_like(acc_up)
 
             @pl.loop(0, rows)
             def _(j):
                 depth = pl.ds(pl.multiple_of(j * width, width), width)
-                x = tok_all[j]
+                x = tok_all[j, span, :]
                 acc_gate[...] += jnp.dot(x, gate_buf[n, depth, :], preferred_element_type=jnp.float32)
                 acc_up[...] += jnp.dot(x, up_buf[n, depth, :], preferred_element_type=jnp.float32)
 
-            @pl.when(e + 1 < local)
+            @pl.when((h == 1) & (e + 1 < local))
             def _():
                 for copy in weight_copies(e + 1, n):
                     copy.start()
 
             cut = pl.ds(pl.multiple_of(n * TILE, TILE), TILE)
-            for s in range(cols):
-                span = pl.ds(s * count, count)
-                v = acc_gate[span, :]
-                h = (v / (1.0 + jnp.exp(-v)) * acc_up[span, :]).astype(jnp.bfloat16)
-                picked = jnp.dot(place[e, s], h, preferred_element_type=jnp.float32)
-                hid[e, r, pl.ds(s * CAP, CAP), cut] = picked.astype(jnp.bfloat16)
+            for i in range(2):
+                lines = pl.ds(i * count, count)
+                v = acc_gate[lines, :]
+                hv = (v / (1.0 + jnp.exp(-v)) * acc_up[lines, :]).astype(jnp.bfloat16)
+                picked = jnp.dot(place[e, first + i], hv, preferred_element_type=jnp.float32)
+                hid[u, r, pl.ds(i * CAP, CAP), cut] = picked.astype(jnp.bfloat16)
 
         @pl.when(has_up)
         def _():
-            hid_copy(0, e, r).start()
+            hid_copy(0, u, r).start()
 
         @pl.when(has_down)
         def _():
-            hid_copy(1, e, r).start()
-
-    def forward(e, d):
+            hid_copy(1, u, r).start()
+
+    def forward(u, d):
         for sign in (-1, 1):
             q = r + sign * d
 
             @pl.when((q >= 0) & (q < rows))
             def _():
-                view = hid.at[e, q]
-                remote(view, view, hid_send.at[0, e, q], hid_recv.at[e, q], c, r).wait_recv()
+                view = hid.at[u, q]
+                remote(view, view, hid_send.at[0, u, q], hid_recv.at[u, q], c, r).wait_recv()
 
                 @pl.when(has_up if sign < 0 else has_down)
                 def _():
-                    hid_copy(0 if sign < 0 else 1, e, q).start()
-
-    def finish(e):
+                    hid_copy(0 if sign < 0 else 1, u, q).start()
+
+    def finish(u):
+        e, h = u // 2, u % 2
+        first = 2 * chip_of(u)
         slot = e % 2
-        down_copy(e, slot).wait()
+
+        @pl.when(h == 0)
+        def _():
+            down_copy(e, slot).wait()
 
         @pl.loop(0, width // TILE)
         def _(n):
             cut = pl.ds(pl.multiple_of(n * TILE, TILE), TILE)
             full = sum(
                 jnp.dot(
-                    hid[e, q], down_buf[slot, pl.ds(q * hidden, hidden), cut],
+                    hid[u, q], down_buf[slot, pl.ds(q * hidden, hidden), cut],
                     preferred_element_type=jnp.float32,
                 )
                 for q in range(rows)
             )
-            for s in range(cols):
-                scaled = full[s * CAP:(s + 1) * CAP] * slot_weight[e, s][:, 0:1]
+            for i in range(2):
+                scale = slot_weight[e, first + i]
+                scaled = full[i * CAP:(i + 1) * CAP] * jnp.concatenate([scale] * (TILE // 128), axis=1)
                 back = jnp.dot(
-                    spread[e, s][:, :CAP], scaled.astype(jnp.bfloat16), preferred_element_type=jnp.float32
+                    spread[e, first + i][:, :CAP], scaled.astype(jnp.bfloat16),
+                    preferred_element_type=jnp.float32,
                 )
-                acc[pl.ds(s * count, count), cut] += back
-
-        @pl.when(e + 2 < local)
+                lines = pl.ds(pl.multiple_of((first + i) * count, count), count)
+                acc[lines, cut] += back
+
+        @pl.when((h == 1) & (e + 2 < local))
         def _():
             down_copy(e + 2, slot).start()
-
-    @pl.loop(0, local + rows - 1)
-    def _(k):
-        @pl.when(k < local)
-        def _():
-            project(k)
-
-        for d in range(1, rows):
-            @pl.when((k >= d) & (k - d < local))
-            def _():
-                forward(k - d, d)
-
-        @pl.when(k >= rows - 1)
-        def _():
-            finish(k - (rows - 1))
 
     def mine(k):
         return acc[pl.ds(pl.multiple_of(col_of[k] * count, count), count), :]
@@ -315,13 +321,45 @@
         dst = (sib_in.at[0], sib_in.at[1], x_in)[i]
         return remote(src, dst, part_send.at[i], part_recv.at[i], col_of[2 if i == 2 else 1], r)
 
-    part[0] = mine(3).astype(jnp.bfloat16)
-    part_copy(0).start()
+    last = units + rows - 2
+
+    @pl.loop(0, last + 1)
+    def _(k):
+        @pl.when(k == 1)
+        def _():
+            pass_on(0)
+            for d in range(1, rows):
+                pass_on(d)
+                if d < rows - 1:
+                    forward(0, d)
+            for q in range(rows):
+                tok_wait(3, q)
+
+        @pl.when(k < units)
+        def _():
+            project(k)
+
+        @pl.when(k == last)
+        def _():
+            part[0] = mine(3).astype(jnp.bfloat16)
+            part_copy(0).start()
+            part_copy(0).wait_recv()
+            x_out[...] = (mine(2) + sib_in[0].astype(jnp.float32)).astype(jnp.bfloat16)
+            part_copy(2).start()
+
+        for d in range(1, rows):
+            least = 0 if d == rows - 1 else 1
+
+            @pl.when((k >= d + least) & (k - d < units))
+            def _():
+                forward(k - d, d)
+
+        @pl.when(k >= rows - 1)
+        def _():
+            finish(k - (rows - 1))
+
     part[1] = mine(1).astype(jnp.bfloat16)
     part_copy(1).start()
-    part_copy(0).wait_recv()
-    x_out[...] = (mine(2) + sib_in[0].astype(jnp.float32)).astype(jnp.bfloat16)
-    part_copy(2).start()
     part_copy(1).wait_recv()
     part_copy(2).wait_recv()
     total = mine(0) + sib_in[1].astype(jnp.float32) + x_in[...].astype(jnp.float32)
@@ -338,13 +376,13 @@
                 @pl.when((has_up & (q <= r)) if kind == 0 else (has_down & (q >= r)))
                 def _():
                     tok_copy(kind, q).wait_send()
-                    for e in range(local):
-                        hid_copy(kind, e, q).wait_send()
+                    for u in range(units):
+                        hid_copy(kind, u, q).wait_send()
 
 
 def scratch(geometry):
     cols, rows, count, picks, local, width, hidden, table = geometry
-    slots, chunks = cols * CAP, hidden // TILE
+    slots, chunks = cols * CAP // 2, hidden // TILE
     bf16, f32 = jnp.bfloat16, jnp.float32
     return [
         ((rows, cols * count, width), bf16),
@@ -352,12 +390,12 @@
         ((chunks, rows * width, TILE), bf16),
         ((chunks, rows * width, TILE), bf16),
         ((2, rows * hidden, width), bf16),
-        ((cols * count, TILE), f32),
-        ((cols * count, TILE), f32),
+        ((2 * count, TILE), f32),
+        ((2 * count, TILE), f32),
         ((local, cols, CAP, count), bf16),
         ((local, cols, count, count), bf16),
         ((local, cols, CAP, 128), f32),
-        ((local, rows, slots, hidden), bf16),
+        ((2 * local, rows, slots, hidden), bf16),
         ((cols * count, width), f32),
         ((2, count, width), bf16),
         ((2, count, width), bf16),
@@ -391,7 +429,7 @@
         scratch_shapes=[pltpu.VMEM(shape, kind) for shape, kind in scratch(geometry)] + [
             dma, dma((chunks,)), dma((chunks,)), dma((2,)),
             dma((3,)), dma((3,)), dma((5, rows)), dma((4, rows)),
-            dma((2, local, rows)), dma((local, rows)), dma((3,)), dma((3,)),
+            dma((2, 2 * local, rows)), dma((2 * local, rows)), dma((3,)), dma((3,)),
         ],
         compiler_params=pltpu.CompilerParams(
             collective_id=0, has_side_effects=True, vmem_limit_bytes=VMEM_BYTES
@@ -407,7 +445,7 @@
     width = tokens.shape[1]
     geometry = (cols, rows, count, picks, local, width, hidden, combine_table.shape[0])
     held = sum(jnp.dtype(kind).itemsize * functools.reduce(lambda a, b: a * b, shape) for shape, kind in scratch(geometry))
-    fits = cols == 4 and hidden % TILE == 0 and width % TILE == 0 and count % 128 == 0 and held < VMEM_BYTES * 9 // 10
+    fits = cols == 4 and rows > 1 and local > 1 and CAP % 16 == 0 and hidden % TILE == 0 and width % TILE == 0 and count % 128 == 0 and held < VMEM_BYTES * 9 // 10
     form = kernel_shards if fits else plain_shards
     return form(tokens, expert_ids, weight_index, combine_table, gate_weight, up_weight, down_weight)
 

time: 174 us -> 164 us (0.943)
  Pallas kernels: 171 us -> 160 us
    pallas_call x1, Pallas kernels: 171 us -> 160 us  [kernel_shards(): pl.pallas_call(functools.partial(expert_kernel, geometry), out_shape=jax....]
where the time goes in v2:
time: 164 us; the launch traced here: 163 us
  Pallas kernels  160 us (98%)
  local copies, waits for them, and re-layouts  1.82 us (1%)
    pallas_call x1, Pallas kernels, kernel_shards(): pl.pallas_call(functools.partial(expert_kernel, geometry), out_shape=jax....  160 us

profile of v2, /device:TPU:0, one launch (start us, length us, event | category | flops | bytes accessed | tf_op | source)
XLA Modules:
  0.0 163.5 jit_solution(10103828354510860150)
XLA Ops:
  0.0 1.3 pad_add_fusion.meta_ref
  1.3 160.3 %shard_map.73 = bf16[128,1792]{1,0:T(8,128)(2,1)} custom-call(bf16[128,1792]{1,0:T(8,128)(2,1)} %tok_hbm.1, s32[16,128]{1,0:T(8,128)} %pad_add_fusion.meta_ref, f32[64]{0:T(128)} %table_ref.1, bf16[4,7168,512]{2,1,0:T(8,128)(2,1)} %gate_hbm.1, bf16[4,7168,512]{2,1,0:T(8,128)(2,1)} %up_hbm.1, bf16[4,2048,1792]{2,1,0:T(8,128)(2,1)} %down_hbm.1), custom_call_target="tpu_custom_call" | custom-call | flops 39460012032 | bytes 88080384 | tf_op jit(solution)/shard_map/pallas_call | solution.py:419
  161.6 1.8 %copy.9 = bf16[128,1792]{1,0:T(8,128)(2,1)} copy(bf16[128,1792]{1,0:T(8,128)(2,1)} %shard_map.73) | data formatting | bytes 917504

commit v3 on v2

--- a/solution.py
+++ b/solution.py
@@ -224,48 +224,75 @@
         own = (u == 0) | ((u >= 2) & (u % 2 == 1))
         return jnp.where(own, chip, 1 - chip)
 
-    def project(u):
-        e, h = u // 2, u % 2
+    def gate(e, s, v, up):
+        h = (v / (1.0 + jnp.exp(-v)) * up).astype(jnp.bfloat16)
+        return jnp.dot(place[e, s], h, preferred_element_type=jnp.float32).astype(jnp.bfloat16)
+
+    def multiply(n, span, lines):
+        acc_gate[lines, :] = jnp.zeros((lines.size, TILE), jnp.float32)
+        acc_up[lines, :] = jnp.zeros((lines.size, TILE), jnp.float32)
+
+        @pl.loop(0, rows)
+        def _(j):
+            depth = pl.ds(pl.multiple_of(j * width, width), width)
+            x = tok_all[j, span, :]
+            acc_gate[lines, :] += jnp.dot(x, gate_buf[n, depth, :], preferred_element_type=jnp.float32)
+            acc_up[lines, :] += jnp.dot(x, up_buf[n, depth, :], preferred_element_type=jnp.float32)
+
+    def fetch_next(e, n):
+        @pl.when(e + 1 < local)
+        def _():
+            for copy in weight_copies(e + 1, n):
+                copy.start()
+
+    def send_own(u):
+        @pl.when(has_up)
+        def _():
+            hid_copy(0, u, r).start()
+
+        @pl.when(has_down)
+        def _():
+            hid_copy(1, u, r).start()
+
+    def project_half(u):
         first = 2 * chip_of(u)
         span = pl.ds(pl.multiple_of(first * count, 2 * count), 2 * count)
 
         @pl.loop(0, chunks)
         def _(n):
-            @pl.when(h == 0)
-            def _():
-                for copy in weight_copies(e, n):
+            @pl.when(u == 0)
+            def _():
+                for copy in weight_copies(0, n):
                     copy.wait()
 
-            acc_gate[...] = jnp.zeros_like(acc_gate)
-            acc_up[...] = jnp.zeros_like(acc_up)
-
-            @pl.loop(0, rows)
-            def _(j):
-                depth = pl.ds(pl.multiple_of(j * width, width), width)
-                x = tok_all[j, span, :]
-                acc_gate[...] += jnp.dot(x, gate_buf[n, depth, :], preferred_element_type=jnp.float32)
-                acc_up[...] += jnp.dot(x, up_buf[n, depth, :], preferred_element_type=jnp.float32)
-
-            @pl.when((h == 1) & (e + 1 < local))
-            def _():
-                for copy in weight_copies(e + 1, n):
-                    copy.start()
+            multiply(n, span, pl.ds(0, 2 * count))
+
+            @pl.when(u == 1)
+            def _():
+                fetch_next(0, n)
 
             cut = pl.ds(pl.multiple_of(n * TILE, TILE), TILE)
             for i in range(2):
                 lines = pl.ds(i * count, count)
-                v = acc_gate[lines, :]
-                hv = (v / (1.0 + jnp.exp(-v)) * acc_up[lines, :]).astype(jnp.bfloat16)
-                picked = jnp.dot(place[e, first + i], hv, preferred_element_type=jnp.float32)
-                hid[u, r, pl.ds(i * CAP, CAP), cut] = picked.astype(jnp.bfloat16)
-
-        @pl.when(has_up)
-        def _():
-            hid_copy(0, u, r).start()
-
-        @pl.when(has_down)
-        def _():
-            hid_copy(1, u, r).start()
+                hid[u, r, pl.ds(i * CAP, CAP), cut] = gate(0, first + i, acc_gate[lines, :], acc_up[lines, :])
+
+        send_own(u)
+
+    def project_whole(e):
+        @pl.loop(0, chunks)
+        def _(n):
+            for copy in weight_copies(e, n):
+                copy.wait()
+            multiply(n, pl.ds(0, cols * count), pl.ds(0, cols * count))
+            fetch_next(e, n)
+            cut = pl.ds(pl.multiple_of(n * TILE, TILE), TILE)
+            for s in range(cols):
+                lines = pl.ds(s * count, count)
+                u = 2 * e + jnp.where(chip == s // 2, 1, 0)
+                hid[u, r, pl.ds((s % 2) * CAP, CAP), cut] = gate(e, s, acc_gate[lines, :], acc_up[lines, :])
+
+        send_own(2 * e)
+        send_own(2 * e + 1)
 
     def forward(u, d):
         for sign in (-1, 1):
@@ -335,9 +362,13 @@
             for q in range(rows):
                 tok_wait(3, q)
 
-        @pl.when(k < units)
-        def _():
-            project(k)
+        @pl.when(k < 2)
+        def _():
+            project_half(k)
+
+        @pl.when((k >= 2) & (k < units) & (k % 2 == 0))
+        def _():
+            project_whole(k // 2)
 
         @pl.when(k == last)
         def _():
@@ -390,8 +421,8 @@
         ((chunks, rows * width, TILE), bf16),
         ((chunks, rows * width, TILE), bf16),
         ((2, rows * hidden, width), bf16),
-        ((2 * count, TILE), f32),
-        ((2 * count, TILE), f32),
+        ((cols * count, TILE), f32),
+        ((cols * count, TILE), f32),
         ((local, cols, CAP, count), bf16),
         ((local, cols, count, count), bf16),
         ((local, cols, CAP, 128), f32),

time: 164 us -> 178 us (1.085)
  Pallas kernels: 160 us -> 174 us
    pallas_call x1, Pallas kernels: 160 us -> 174 us  [kernel_shards(): pl.pallas_call(functools.partial(expert_kernel, geometry), out_shape=jax....]
where the time goes in v3:
time: 178 us; the launch traced here: 177 us
  Pallas kernels  174 us (98%)
  local copies, waits for them, and re-layouts  1.82 us (1%)
    pallas_call x1, Pallas kernels, kernel_shards(): pl.pallas_call(functools.partial(expert_kernel, geometry), out_shape=jax....  174 us

profile of v3, /device:TPU:0, one launch (start us, length us, event | category | flops | bytes accessed | tf_op | source)
XLA Modules:
  0.0 177.3 jit_solution(918166421853254034)
XLA Ops:
  0.0 1.3 pad_add_fusion.meta_ref
  1.3 174.2 %shard_map.73 = bf16[128,1792]{1,0:T(8,128)(2,1)} custom-call(bf16[128,1792]{1,0:T(8,128)(2,1)} %tok_hbm.1, s32[16,128]{1,0:T(8,128)} %pad_add_fusion.meta_ref, f32[64]{0:T(128)} %table_ref.1, bf16[4,7168,512]{2,1,0:T(8,128)(2,1)} %gate_hbm.1, bf16[4,7168,512]{2,1,0:T(8,128)(2,1)} %up_hbm.1, bf16[4,2048,1792]{2,1,0:T(8,128)(2,1)} %down_hbm.1), custom_call_target="tpu_custom_call" | custom-call | flops 39460012032 | bytes 88080384 | tf_op jit(solution)/shard_map/pallas_call | solution.py:450
  175.5 1.8 %copy.9 = bf16[128,1792]{1,0:T(8,128)(2,1)} copy(bf16[128,1792]{1,0:T(8,128)(2,1)} %shard_map.73) | data formatting | bytes 917504
